TPU v7x, 256 devices: a whole 4x4x8 slice. The times are simulated.
256 devices in a mesh: dp: 16 (over z, core), seq: 16 (over x, y).
Axes of the slice: x: 4, y: 4, z: 8, core: 2. Of those that a mesh axis runs over, the one named last changes fastest.
Arguments:
- queries: bfloat16 [16, 2048, 2560], P('dp', 'seq'), may hold values from -24 to 24
- keys: bfloat16 [16, 2048, 2560], P('dp', 'seq'), may hold values from -24 to 24
- values: bfloat16 [16, 2048, 2560], P('dp', 'seq'), may hold values from -6 to 6
- block_masks: int32 [2, 16, 16], replicated, may hold values from 0 to 1, as said below
- head_kind: int32 [20], replicated, may hold values from 0 to 1
- out_weight: bfloat16 [2560, 5120], P(None, 'dp'), may hold values from -0.125 to 0.125
Outputs:
- attended: bfloat16 [16, 2048, 5120], P('dp', 'seq')
Inputs may be any that keep to these rules, and one draw needn't show every extreme that they name: block_masks[0, i, j] is 1 wherever blocks i and j lie in the same frame of 4 blocks, block_masks[1, i, j] wherever i - j is a multiple of 4; the other entries are 0 or 1.
All inputs are finite; a program needn't handle non-finite values.
Results may differ from a plain program's by a relative error of at most 0.0057.
Values may be sent and summed in bfloat16 or wider, within the bound.
A program may use at most 128 MiB of HBM per device.

v0:
```python
import math

import jax
import jax.numpy as jnp
from jax import lax
from jax.sharding import PartitionSpec as P

HEAD_DIM = 128


def attend(rows_query, row_start, key_rows, value_rows, allowed):
    count, width = rows_query.shape
    length = key_rows.shape[0]
    blocks = allowed.shape[1]
    block = length // blocks
    step = min(512, count)
    scale = 1.0 / math.sqrt(width)

    def one_block(index):
        start = index * step
        query_block = lax.dynamic_slice_in_dim(rows_query, start, step, 0)
        scores = (
            lax.dot_general(
                query_block, key_rows, (((1,), (1,)), ((), ())), preferred_element_type=jnp.float32
            )
            * scale
        )
        window = lax.dynamic_slice_in_dim(allowed, (row_start + start) // block, step // block, 0)
        tiles = scores.reshape(step // block, block, blocks, block)
        tiles = jnp.where(window[:, None, :, None] == 1, tiles, -jnp.inf)
        scores = tiles.reshape(step, length)
        largest = jnp.max(scores, axis=1, keepdims=True)
        powers = jnp.exp(scores - largest)
        weights = (powers / jnp.sum(powers, axis=1, keepdims=True)).astype(jnp.bfloat16)
        return jnp.dot(weights, value_rows, preferred_element_type=jnp.float32).astype(jnp.bfloat16)

    outputs = lax.map(one_block, jnp.arange(count // step, dtype=jnp.int32))
    return outputs.reshape(count, width)


def select_mask(block_masks, head_kind, head_id):
    heads = head_kind.shape[0]
    match = (jnp.arange(heads, dtype=jnp.int32) == head_id).astype(jnp.int32)
    kind = jnp.sum(match * head_kind)
    return jnp.where(kind == 0, block_masks[0], block_masks[1])


def group_attention(query_slots, key_slots, value_slots, block_masks, head_kind, groups, position):
    results = []
    for slot in range(query_slots.shape[1]):
        allowed = select_mask(block_masks, head_kind, slot * groups + position)
        results.append(
            attend(
                query_slots[:, slot, 0], 0, key_slots[:, slot, 0], value_slots[:, slot, 0], allowed
            )
        )
    return jnp.stack(results, axis=1)[:, :, None, :]


def per_device(queries, keys, values, block_masks, head_kind, out_weight):
    local_rows = queries.shape[1]
    head_size = HEAD_DIM
    heads = head_kind.shape[0]
    groups = lax.axis_size("seq")
    position = lax.axis_index("seq")
    query_heads = queries[0].reshape(local_rows, heads, head_size)
    key_heads = keys[0].reshape(local_rows, heads, head_size)
    value_heads = values[0].reshape(local_rows, heads, head_size)
    slots = -(-heads // groups)
    padding = slots * groups - heads

    def arrange(source):
        return jnp.pad(source, ((0, 0), (0, padding), (0, 0))).reshape(
            local_rows, slots, groups, head_size
        )

    query_slots, key_slots, value_slots = (
        lax.all_to_all(arrange(query_heads), "seq", split_axis=2, concat_axis=0, tiled=True),
        lax.all_to_all(arrange(key_heads), "seq", split_axis=2, concat_axis=0, tiled=True),
        lax.all_to_all(arrange(value_heads), "seq", split_axis=2, concat_axis=0, tiled=True),
    )
    stacked = group_attention(
        query_slots, key_slots, value_slots, block_masks, head_kind, groups, position
    )
    returned = lax.all_to_all(stacked, "seq", split_axis=0, concat_axis=2, tiled=True)
    heads_out = returned.reshape(local_rows, slots * groups * head_size)[:, : heads * head_size]
    attended = jnp.dot(
        heads_out,
        lax.all_gather(out_weight, "dp", axis=1, tiled=True),
        preferred_element_type=jnp.float32,
    ).astype(jnp.bfloat16)
    return attended[None]


def solution(mesh):
    placed = (
        P("dp", "seq", None),
        P("dp", "seq", None),
        P("dp", "seq", None),
        P(),
        P(),
        P(None, "dp"),
    )
    return jax.shard_map(
        per_device, mesh=mesh, in_specs=placed, out_specs=P("dp", "seq", None), check_vma=False
    )
```

profile of v0, /device:TPU:1, one launch (start us, length us, event | category | flops | bytes accessed | tf_op | source)
XLA Modules:
  0.0 174.9 jit_solution(10759134442349916956)
XLA Ops:
  7.3 1.4 copy.34
  9.9 7.7 %all-to-all-start.1 = ((bf16[128,2,16,128]{0,3,1,2:T(8,128)(2,1)}), bf16[128,2,16,128]{0,3,1,2:T(8,128)(2,1)S(1)}, u32[]{:S(2)}, u32[]{:S(2)}) async-start(bf16[128,2,16,128]{0,3,1,2:T(8,128)(2,1)} %copy.35), calls=%async_computation.1 | async-start | bytes 2097152 | tf_op jit(solution)/shard_map/all_to_all | solution.py:79
  19.1 14.0 %all-to-all-done.1 = bf16[128,2,16,128]{0,3,1,2:T(8,128)(2,1)S(1)} async-done(((bf16[128,2,16,128]{0,3,1,2:T(8,128)(2,1)}), bf16[128,2,16,128]{0,3,1,2:T(8,128)(2,1)S(1)}, u32[]{:S(2)}, u32[]{:S(2)}) %all-to-all-start.1) | async-done | bytes 1048608 | tf_op jit(solution)/shard_map/all_to_all | solution.py:79
  33.1 4.1 %all-to-all-start.2 = ((bf16[128,2,16,128]{0,3,1,2:T(8,128)(2,1)}), bf16[128,2,16,128]{0,3,1,2:T(8,128)(2,1)S(1)}, u32[]{:S(2)}, u32[]{:S(2)}) async-start(bf16[128,2,16,128]{0,3,1,2:T(8,128)(2,1)} %copy.38), calls=%async_computation.2 | async-start | bytes 2097152 | tf_op jit(solution)/shard_map/all_to_all | solution.py:80
  38.7 12.9 %all-to-all-done.2 = bf16[128,2,16,128]{0,3,1,2:T(8,128)(2,1)S(1)} async-done(((bf16[128,2,16,128]{0,3,1,2:T(8,128)(2,1)}), bf16[128,2,16,128]{0,3,1,2:T(8,128)(2,1)S(1)}, u32[]{:S(2)}, u32[]{:S(2)}) %all-to-all-start.2) | async-done | bytes 1048608 | tf_op jit(solution)/shard_map/all_to_all | solution.py:80
  51.6 5.2 %all-to-all-start = ((bf16[128,2,16,128]{0,3,1,2:T(8,128)(2,1)}), bf16[128,2,16,128]{0,3,1,2:T(8,128)(2,1)S(1)}, u32[]{:S(2)}, u32[]{:S(2)}) async-start(bf16[128,2,16,128]{0,3,1,2:T(8,128)(2,1)} %copy.32), calls=%async_computation | async-start | bytes 2097152 | tf_op jit(solution)/shard_map/all_to_all | solution.py:78
  58.7 1.3 copy.36
  60.1 1.3 copy.39
  61.3 10.2 %all-to-all-done = bf16[128,2,16,128]{0,3,1,2:T(8,128)(2,1)S(1)} async-done(((bf16[128,2,16,128]{0,3,1,2:T(8,128)(2,1)}), bf16[128,2,16,128]{0,3,1,2:T(8,128)(2,1)S(1)}, u32[]{:S(2)}, u32[]{:S(2)}) %all-to-all-start) | async-done | bytes 1048608 | tf_op jit(solution)/shard_map/all_to_all | solution.py:78
  72.3 2.5 %slice_bitcast_fusion.3 = (bf16[2048,128]{1,0:T(8,128)(2,1)S(1)}, bf16[2048,128]{1,0:T(8,128)(2,1)}, bf16[2048,128]{1,0:T(8,128)(2,1)}, bf16[2048,128]{1,0:T(8,128)(2,1)}) fusion(bf16[2048,2,1,128]{3,0,1,2:T(8,128)(2,1)} %bitcast.98, bf16[2048,2,1,128]{3,0,1,2:T(8,128)(2,1)S(1)} %bitcast.97), kind=kLoop, calls=%fused_computation.29 | loop fusion | bytes 4194304 | tf_op jit(solution)/shard_map/squeeze | solution.py:54
  74.9 22.3 %while.24 = (s32[]{:T(128)}, bf16[4,512,128]{2,1,0:T(8,128)(2,1)S(1)}, s32[4]{0:T(128)S(1)}, s32[16,16]{1,0:T(8,128)S(1)}, bf16[2048,128]{1,0:T(8,128)(2,1)S(1)}...) while((s32[]{:T(128)}, ...), condition=%wide.region_4.5_spmd, body=%wide.region_1.4_spmd.sunk | while | flops 545324160 | bytes 16001794 | solution.py:37
  76.6 2.2 %fusion.37 = (f32[512]{0:T(512)S(1)}, f32[512,2048]{1,0:T(8,128)S(1)}) fusion(bf16[2048,128]{1,0:T(8,128)(2,1)} %get-tuple-element.405, bf16[2048,128]{1,0:T(8,128)(2,1)S(1)} %get-tuple-element.404, s32[]{:T(128)S(6)} %select_n.91, pred[64,8,16,128]{3,2,1,0:T(8,128)(4,1)S(1)} %bitcast.90), kind=kOutput, calls=%fused_computation.38.clone.1 | convolution fusion | flops 271580672 | bytes 5900292 | tf_op jit(solution)/shard_map/while/body/eval_jaxpr/dot_general | solution.py:23
  82.3 2.1 %fusion.37 = (f32[512]{0:T(512)S(1)}, f32[512,2048]{1,0:T(8,128)S(1)}) fusion(bf16[2048,128]{1,0:T(8,128)(2,1)} %get-tuple-element.405, bf16[2048,128]{1,0:T(8,128)(2,1)S(1)} %get-tuple-element.404, s32[]{:T(128)S(6)} %select_n.91, pred[64,8,16,128]{3,2,1,0:T(8,128)(4,1)S(1)} %bitcast.90), kind=kOutput, calls=%fused_computation.38.clone.1 | convolution fusion | flops 271580672 | bytes 5900292 | tf_op jit(solution)/shard_map/while/body/eval_jaxpr/dot_general | solution.py:23
  87.9 2.1 %fusion.37 = (f32[512]{0:T(512)S(1)}, f32[512,2048]{1,0:T(8,128)S(1)}) fusion(bf16[2048,128]{1,0:T(8,128)(2,1)} %get-tuple-element.405, bf16[2048,128]{1,0:T(8,128)(2,1)S(1)} %get-tuple-element.404, s32[]{:T(128)S(6)} %select_n.91, pred[64,8,16,128]{3,2,1,0:T(8,128)(4,1)S(1)} %bitcast.90), kind=kOutput, calls=%fused_computation.38.clone.1 | convolution fusion | flops 271580672 | bytes 5900292 | tf_op jit(solution)/shard_map/while/body/eval_jaxpr/dot_general | solution.py:23
  93.4 2.1 %fusion.37 = (f32[512]{0:T(512)S(1)}, f32[512,2048]{1,0:T(8,128)S(1)}) fusion(bf16[2048,128]{1,0:T(8,128)(2,1)} %get-tuple-element.405, bf16[2048,128]{1,0:T(8,128)(2,1)S(1)} %get-tuple-element.404, s32[]{:T(128)S(6)} %select_n.91, pred[64,8,16,128]{3,2,1,0:T(8,128)(4,1)S(1)} %bitcast.90), kind=kOutput, calls=%fused_computation.38.clone.1 | convolution fusion | flops 271580672 | bytes 5900292 | tf_op jit(solution)/shard_map/while/body/eval_jaxpr/dot_general | solution.py:23
  97.3 22.1 %while.25 = (s32[]{:T(128)}, bf16[4,512,128]{2,1,0:T(8,128)(2,1)S(1)}, s32[4]{0:T(128)S(1)}, s32[16,16]{1,0:T(8,128)S(1)}, bf16[2048,128]{1,0:T(8,128)(2,1)S(1)}...) while((s32[]{:T(128)}, ...), condition=%wide.region_9.10_spmd, body=%wide.region_6.9_spmd.sunk | while | flops 545324160 | bytes 18098972 | solution.py:37
  99.0 2.2 %fusion.42 = (f32[512]{0:T(512)S(1)}, f32[512,2048]{1,0:T(8,128)S(1)}) fusion(bf16[2048,128]{1,0:T(8,128)(2,1)} %get-tuple-element.360, bf16[2048,128]{1,0:T(8,128)(2,1)S(1)} %get-tuple-element.359, s32[]{:T(128)S(6)} %select_n.94, pred[64,8,16,128]{3,2,1,0:T(8,128)(4,1)S(1)} %bitcast.91), kind=kOutput, calls=%fused_computation.39.clone.1 | convolution fusion | flops 271580672 | bytes 5900292 | tf_op jit(solution)/shard_map/while/body/eval_jaxpr/dot_general | solution.py:23
  104.5 2.2 %fusion.42 = (f32[512]{0:T(512)S(1)}, f32[512,2048]{1,0:T(8,128)S(1)}) fusion(bf16[2048,128]{1,0:T(8,128)(2,1)} %get-tuple-element.360, bf16[2048,128]{1,0:T(8,128)(2,1)S(1)} %get-tuple-element.359, s32[]{:T(128)S(6)} %select_n.94, pred[64,8,16,128]{3,2,1,0:T(8,128)(4,1)S(1)} %bitcast.91), kind=kOutput, calls=%fused_computation.39.clone.1 | convolution fusion | flops 271580672 | bytes 5900292 | tf_op jit(solution)/shard_map/while/body/eval_jaxpr/dot_general | solution.py:23
  110.0 2.2 %fusion.42 = (f32[512]{0:T(512)S(1)}, f32[512,2048]{1,0:T(8,128)S(1)}) fusion(bf16[2048,128]{1,0:T(8,128)(2,1)} %get-tuple-element.360, bf16[2048,128]{1,0:T(8,128)(2,1)S(1)} %get-tuple-element.359, s32[]{:T(128)S(6)} %select_n.94, pred[64,8,16,128]{3,2,1,0:T(8,128)(4,1)S(1)} %bitcast.91), kind=kOutput, calls=%fused_computation.39.clone.1 | convolution fusion | flops 271580672 | bytes 5900292 | tf_op jit(solution)/shard_map/while/body/eval_jaxpr/dot_general | solution.py:23
  115.5 2.2 %fusion.42 = (f32[512]{0:T(512)S(1)}, f32[512,2048]{1,0:T(8,128)S(1)}) fusion(bf16[2048,128]{1,0:T(8,128)(2,1)} %get-tuple-element.360, bf16[2048,128]{1,0:T(8,128)(2,1)S(1)} %get-tuple-element.359, s32[]{:T(128)S(6)} %select_n.94, pred[64,8,16,128]{3,2,1,0:T(8,128)(4,1)S(1)} %bitcast.91), kind=kOutput, calls=%fused_computation.39.clone.1 | convolution fusion | flops 271580672 | bytes 5900292 | tf_op jit(solution)/shard_map/while/body/eval_jaxpr/dot_general | solution.py:23
  119.5 8.7 %copy.40 = bf16[2048,2,1,128]{3,1,2,0:T(2,128)(2,1)S(1)} copy(bf16[2048,2,1,128]{3,0,1,2:T(8,128)(2,1)S(1)} %maximum_bitcast_fusion) | data formatting | bytes 2097152 | tf_op jit(solution)/shard_map/broadcast_in_dim | solution.py:57
  128.2 19.2 %all_to_all.69 = bf16[2048,2,1,128]{3,1,2,0:T(2,128)(2,1)S(1)} all-to-all(bf16[2048,2,1,128]{3,1,2,0:T(2,128)(2,1)S(1)} %copy.40), channel_id=1, replica_groups=mesh['dp'=16,'seq'=16] {'seq'}, dimensions={0} | all-to-all | bytes 2097152 | tf_op jit(solution)/shard_map/all_to_all | solution.py:85
  148.2 5.1 %all-gather.2.cloned.1.call-done = bf16[2560,5120]{0,1:T(8,128)(2,1)} async-done(((bf16[2560,320]{0,1:T(8,128)(2,1)}), bf16[2560,5120]{0,1:T(8,128)(2,1)}) %all-gather.2.cloned.1.call-update) | async-done | bytes 26214416 | tf_op jit(solution)/shard_map/all_gather | solution.py:89
  153.3 14.8 %fusion.14 = bf16[1,128,5120]{2,1,0:T(8,128)(2,1)} fusion(bf16[2560,5120]{0,1:T(8,128)(2,1)} %all-gather.2.cloned.1.call-done, bf16[128,4096]{0,1:T(8,128)(2,1)S(1)} %bitcast.99), kind=kOutput, calls=%fused_computation.23 | convolution fusion | flops 3356098560 | bytes 28180480 | tf_op jit(solution)/shard_map/dot_general | solution.py:87
  (79 shorter events, 28.5 us)
Async XLA Ops:
  6.5 11.1 %copy-start.1 = (bf16[1,128,2560]{2,1,0:T(8,128)(2,1)S(1)}, bf16[1,128,2560]{2,1,0:T(8,128)(2,1)}, u32[]{:S(2)}) copy-start(bf16[1,128,2560]{2,1,0:T(8,128)(2,1)} %param.12) | copy-start | bytes 1966084
  6.5 146.8 %all-gather.2.cloned.1.call-start = ((), (), s32[]{:S(2)}) async-start(), calls=%async_computation.4 | async-start | bytes 27852800 | tf_op jit(solution)/shard_map/all_gather | solution.py:89
  9.9 27.3 %copy-start.2 = (bf16[1,128,2560]{2,1,0:T(8,128)(2,1)S(1)}, bf16[1,128,2560]{2,1,0:T(8,128)(2,1)}, u32[]{:S(2)}) copy-start(bf16[1,128,2560]{2,1,0:T(8,128)(2,1)} %param.10) | copy-start | bytes 1966084
  9.9 23.2 %all-to-all-start.1 = ((bf16[128,2,16,128]{0,3,1,2:T(8,128)(2,1)}), bf16[128,2,16,128]{0,3,1,2:T(8,128)(2,1)S(1)}, u32[]{:S(2)}, u32[]{:S(2)}) async-start(bf16[128,2,16,128]{0,3,1,2:T(8,128)(2,1)} %copy.35), calls=%async_computation.1 | async-start | bytes 2097152 | tf_op jit(solution)/shard_map/all_to_all | solution.py:79
  19.1 37.6 %copy-start.5 = (s32[20]{0:T(128)S(1)}, s32[20]{0:T(128)}, u32[]{:S(2)}) copy-start(s32[20]{0:T(128)} %param.14) | copy-start | bytes 244
  19.1 39.6 %copy-start.4 = (s32[2,16,16]{2,1,0:T(8,128)S(1)}, s32[2,16,16]{2,1,0:T(8,128)}, u32[]{:S(2)}) copy-start(s32[2,16,16]{2,1,0:T(8,128)} %param.13) | copy-start | bytes 6148
  33.1 18.5 %all-to-all-start.2 = ((bf16[128,2,16,128]{0,3,1,2:T(8,128)(2,1)}), bf16[128,2,16,128]{0,3,1,2:T(8,128)(2,1)S(1)}, u32[]{:S(2)}, u32[]{:S(2)}) async-start(bf16[128,2,16,128]{0,3,1,2:T(8,128)(2,1)} %copy.38), calls=%async_computation.2 | async-start | bytes 2097152 | tf_op jit(solution)/shard_map/all_to_all | solution.py:80
  51.6 20.0 %all-to-all-start = ((bf16[128,2,16,128]{0,3,1,2:T(8,128)(2,1)}), bf16[128,2,16,128]{0,3,1,2:T(8,128)(2,1)S(1)}, u32[]{:S(2)}, u32[]{:S(2)}) async-start(bf16[128,2,16,128]{0,3,1,2:T(8,128)(2,1)} %copy.32), calls=%async_computation | async-start | bytes 2097152 | tf_op jit(solution)/shard_map/all_to_all | solution.py:78
  61.3 10.9 %copy-start = (bf16[128,2,16,128]{3,0,2,1:T(8,128)(2,1)S(1)}, bf16[128,2,16,128]{3,0,2,1:T(8,128)(2,1)}, u32[]{:S(2)}) copy-start(bf16[128,2,16,128]{3,0,2,1:T(8,128)(2,1)} %copy.36) | copy-start | bytes 3145732
  99.0 2.9 %copy-start.3 = (bf16[2048,128]{1,0:T(8,128)(2,1)S(1)}, bf16[2048,128]{1,0:T(8,128)(2,1)}, u32[]{:S(2)}) copy-start(bf16[2048,128]{1,0:T(8,128)(2,1)} %get-tuple-element.361) | copy-start | bytes 1572868 | tf_op jit(solution)/shard_map/while
  104.5 2.9 %copy-start.3 = (bf16[2048,128]{1,0:T(8,128)(2,1)S(1)}, bf16[2048,128]{1,0:T(8,128)(2,1)}, u32[]{:S(2)}) copy-start(bf16[2048,128]{1,0:T(8,128)(2,1)} %get-tuple-element.361) | copy-start | bytes 1572868 | tf_op jit(solution)/shard_map/while
  110.0 2.9 %copy-start.3 = (bf16[2048,128]{1,0:T(8,128)(2,1)S(1)}, bf16[2048,128]{1,0:T(8,128)(2,1)}, u32[]{:S(2)}) copy-start(bf16[2048,128]{1,0:T(8,128)(2,1)} %get-tuple-element.361) | copy-start | bytes 1572868 | tf_op jit(solution)/shard_map/while
  115.5 2.9 %copy-start.3 = (bf16[2048,128]{1,0:T(8,128)(2,1)S(1)}, bf16[2048,128]{1,0:T(8,128)(2,1)}, u32[]{:S(2)}) copy-start(bf16[2048,128]{1,0:T(8,128)(2,1)} %get-tuple-element.361) | copy-start | bytes 1572868 | tf_op jit(solution)/shard_map/while
Sparse Core Ops, SparseCore 0:
  9.2 144.0 all-gather.1
where the time goes:
time: 176 us; the launch traced here: 175 us
  waiting for transfers between devices  42.9 us (24%)
  matrix products  39.6 us (22%)
  local copies, waits for them, and re-layouts  28.9 us (16%)
  blocking collectives  19.2 us (11%)
  starting transfers between devices  16.9 us (10%)
  between operations  14.9 us (8%)
  other arithmetic  6.61 us (4%)
  loops' own time  5.96 us (3%)
    all_to_all x1, blocking collectives, per_device(): lax.all_to_all(stacked, 'seq', split_axis=0, concat_axis=2, tiled=True)  19.2 us
    dot_general x8, matrix products, one_block(): lax.dot_general(query_block, key_rows, (((1,), (1,)), ((), ())), preferre...  17.3 us
    dot_general x1, matrix products, per_device(): jnp.dot(heads_out, lax.all_gather(out_weight, 'dp', axis=1, tiled=True),...  14.8 us
    all_to_all x1, waiting for transfers between devices, per_device(): lax.all_to_all(arrange(key_heads), 'seq', split_axis=2, concat_axis=0, ti...  14 us
    all_to_all x1, waiting for transfers between devices, per_device(): lax.all_to_all(arrange(value_heads), 'seq', split_axis=2, concat_axis=0,...  12.9 us
    all_to_all x1, waiting for transfers between devices, per_device(): lax.all_to_all(arrange(query_heads), 'seq', split_axis=2, concat_axis=0,...  10.2 us
    broadcast_in_dim x1, local copies, waits for them, and re-layouts, group_attention(): return jnp.stack(results, axis=1)[:, :, None, :]  8.68 us
    all_to_all x1, starting transfers between devices, per_device(): lax.all_to_all(arrange(key_heads), 'seq', split_axis=2, concat_axis=0, ti...  7.72 us
  transfers between devices with their start and end apart: 4, of which 4 were waited for; matrix products, arithmetic and copies ran while one was open for 34% of the time, Pallas kernels for 0%

commit v1 on v0

v1 whole, which is shorter than its diff:
```python
import functools
import math

import jax
import jax.numpy as jnp
from jax import lax
from jax.experimental import pallas as pl
from jax.experimental.pallas import tpu as pltpu
from jax.sharding import PartitionSpec as P

HD = 128
SIDE = 4
PLANE = 16
DEPTH = 8
HEADS = 20
EXTRA = HEADS - PLANE
SEQ = 2048
ROWS = 128
K = 2560
KQ = K // SIDE
NB = 320
RB = 112
RC = NB - 2 * RB
RH = 64
RCH = RC // 2
QB = 256
NC = 256
MESH = pl.DeviceIdType.MESH
SCALE = math.log2(math.e) / math.sqrt(HD)


def rcopy(src, dst, send, recv, device):
    return pltpu.make_async_remote_copy(
        src_ref=src, dst_ref=dst, send_sem=send, recv_sem=recv,
        device_id=device, device_id_type=MESH,
    )


def arrived(ref, sem):
    pltpu.make_async_copy(ref, ref, sem).wait()


def al(value, unit):
    return pl.multiple_of(value, unit)


def kernel(q_in, k_in, v_in, masks, kinds, w_in, out,
           qb, kb, vb, bias, ob, xb, wb, yb, ys,
           zb_sem, zc_sem, x1_sem, x2_sem, a_sem, o_sem, s_sem, y_sem,
           w_send, a_send, o_send, s_send, y_send, l_sem):
    dp = lax.axis_index("dp")
    me = lax.axis_index("seq")
    z, c = dp // 2, dp % 2
    xi, yi = me // SIDE, me % SIDE
    sib = (z * 2 + 1 - c, me)
    up = (((z + 1) % DEPTH) * 2 + c, me)
    down = (((z + DEPTH - 1) % DEPTH) * 2 + c, me)
    near = (
        ((dp, ((xi + 1) % SIDE) * SIDE + yi), (dp, ((xi + 3) % SIDE) * SIDE + yi)),
        ((dp, xi * SIDE + (yi + 1) % SIDE), (dp, xi * SIDE + (yi + 3) % SIDE)),
    )
    coord = (xi, yi)
    extra = me % 5 == 0
    head1 = PLANE + me // 5

    barrier = pltpu.get_barrier_semaphore()

    @pl.loop(1, PLANE)
    def _(d):
        pl.semaphore_signal(barrier, inc=1, device_id=(dp, (me + d) % PLANE), device_id_type=MESH)

    for device in (up, down, sib):
        pl.semaphore_signal(barrier, inc=1, device_id=device, device_id_type=MESH)
    pl.semaphore_wait(barrier, PLANE + 2)

    def piece(block, kind, quarter, first=0, rows=RB):
        start = al(((z + block) % DEPTH) * NB + kind * RB + first, 16)
        return wb.at[pl.ds(start, rows), pl.ds(al(quarter * KQ, HD), KQ)]

    def deep(block, first, rows):
        start = al(((z + block) % DEPTH) * NB + 2 * RB + first, 16)
        return wb.at[pl.ds(start, rows), :]

    own = pltpu.make_async_copy(w_in, wb.at[pl.ds(al(z * NB, 16), NB), :], l_sem)
    own.start()

    for kind in range(2):
        src = w_in.at[kind * RB:(kind + 1) * RB, pl.ds(al(coord[kind] * KQ, HD), KQ)]
        for way, device in enumerate((up, down)):
            rcopy(src, piece(DEPTH, kind, coord[kind]), w_send, zb_sem.at[0, way, kind], device).start()

    sources = (k_in, q_in, v_in)

    def landing(which, slot, block):
        rows = pl.ds(al(block * ROWS, ROWS), ROWS)
        if which == 2:
            return vb.at[slot, rows, 0:HD]
        return (kb, qb)[which].at[slot, rows, :]

    def whole(which, slot):
        if which == 2:
            return vb.at[slot, :, 0:HD]
        return (kb, qb)[which].at[slot]

    def columns(which, head):
        return sources[which].at[:, pl.ds(al(head * HD, HD), HD)]

    @pl.loop(1, PLANE)
    def _(d):
        to = (me + d) % PLANE
        for which in range(3):
            rcopy(columns(which, to), landing(which, 0, me), a_send, a_sem.at[which, 0], (dp, to)).start()

    for which in range(3):
        pltpu.make_async_copy(columns(which, me), landing(which, 0, me), a_sem.at[which, 0]).start()

    @pl.loop(0, EXTRA)
    def _(j):
        for which in range(3):
            @pl.when(me != 5 * j)
            def _():
                rcopy(columns(which, PLANE + j), landing(which, 1, me), a_send,
                      a_sem.at[which, 1], (dp, 5 * j)).start()

            @pl.when(me == 5 * j)
            def _():
                pltpu.make_async_copy(columns(which, PLANE + j), landing(which, 1, me),
                                      a_sem.at[which, 1]).start()

    for slot in range(2):
        kind = kinds[me if slot == 0 else jnp.where(extra, head1, me)]
        allowed = jnp.where(kind == 0, masks[0], masks[1])
        for block in range(SEQ // HD):
            column = jnp.where(allowed[:, block:block + 1] == 1, 0.0, -jnp.inf)
            bias[slot, :, block * HD:(block + 1) * HD] = jnp.broadcast_to(column, (SEQ // HD, HD))
        vb[slot, :, HD:] = jnp.ones((SEQ, HD), jnp.bfloat16)

    def first_hop(block, slot):
        for kind in range(2):
            for way, device in enumerate(near[kind]):
                part = piece(block, kind, coord[kind])
                rcopy(part, part, w_send, x1_sem.at[slot, kind, way], device).start()

    def second_hop(block, slot):
        for kind in range(2):
            back, ahead = (coord[kind] + 3) % SIDE, (coord[kind] + 1) % SIDE
            arrived(piece(block, kind, back), x1_sem.at[slot, kind, 0])
            part = piece(block, kind, back, 0, RH)
            rcopy(part, part, w_send, x2_sem.at[slot, kind, 0], near[kind][0]).start()
            arrived(piece(block, kind, ahead), x1_sem.at[slot, kind, 1])
            part = piece(block, kind, ahead, RH, RB - RH)
            rcopy(part, part, w_send, x2_sem.at[slot, kind, 1], near[kind][1]).start()

    def last_hop(block, slot):
        for kind in range(2):
            far = (coord[kind] + 2) % SIDE
            arrived(piece(block, kind, far, 0, RH), x2_sem.at[slot, kind, 0])
            arrived(piece(block, kind, far, RH, RB - RH), x2_sem.at[slot, kind, 1])

    blocks = (7, 1, 6, 2, 5, 3, 4)

    def along_z(step):
        for way in range(2):
            block = (DEPTH - step, step)[way]
            for kind in range(2):
                arrived(piece(block, kind, coord[kind]), zb_sem.at[step - 1, way, kind])
                if step < 3 or kind == way:
                    part = piece(block, kind, coord[kind])
                    rcopy(part, part, w_send, zb_sem.at[step, way, kind], (up, down)[way]).start()
            first_hop(block, 2 * (step - 1) + way)

    def deep_z(step):
        for way in range(2):
            block = (DEPTH - step, step)[way]
            arrived(deep(block, 0, RC), zc_sem.at[step - 1, way])
            part = deep(block, 0, RC) if step < 3 else deep(block, way * RCH, RCH)
            rcopy(part, part, w_send, zc_sem.at[step, way], (up, down)[way]).start()

    along_z(1)
    along_z(2)
    along_z(3)
    for way, device in enumerate((up, down)):
        rcopy(w_in.at[2 * RB:NB, :], deep(DEPTH, 0, RC), w_send, zc_sem.at[0, way], device).start()
    for kind in range(2):
        arrived(piece(4, kind, coord[kind]), zb_sem.at[3, kind, kind])
    first_hop(4, 6)

    def attention(slot, head, low, high):
        @pl.loop(low, high)
        def _(i):
            turn = (i + me // 2) % (SEQ // QB)
            rows = pl.ds(al(turn * QB, QB), QB)
            scores = lax.dot_general(qb[slot, rows, :], kb[slot], (((1,), (1,)), ((), ())),
                                     preferred_element_type=jnp.float32)
            powers = []
            for half in range(QB // ROWS):
                part = scores[half * ROWS:(half + 1) * ROWS] + bias[slot, pl.ds(turn * 2 + half, 1), :]
                largest = jnp.max(part, axis=1, keepdims=True)
                powers.append(jnp.exp2((part - largest) * SCALE).astype(jnp.bfloat16))
            total = jnp.dot(jnp.concatenate(powers, axis=0), vb[slot], preferred_element_type=jnp.float32)
            ob[slot, rows, :] = (total[:, :HD] / total[:, HD:]).astype(jnp.bfloat16)
            for half in range(QB // ROWS):
                to = turn * 2 + half
                src = ob.at[slot, pl.ds(al(to * ROWS, ROWS), ROWS), :]
                dst = xb.at[0, :, pl.ds(al(head * HD, HD), HD)]

                @pl.when(to != me)
                def _():
                    rcopy(src, dst, o_send, o_sem, (dp, to)).start()

                @pl.when(to == me)
                def _():
                    pltpu.make_async_copy(src, dst, o_sem).start()

    for which in range(3):
        arrived(whole(which, 0), a_sem.at[which, 0])
    attention(0, me, 0, 4)
    second_hop(blocks[0], 0)
    second_hop(blocks[1], 1)
    deep_z(1)
    attention(0, me, 4, 8)
    second_hop(blocks[2], 2)
    second_hop(blocks[3], 3)

    @pl.when(extra)
    def _():
        for which in range(3):
            arrived(whole(which, 1), a_sem.at[which, 1])
        attention(1, head1, 0, 8)

    deep_z(2)
    second_hop(blocks[4], 4)
    second_hop(blocks[5], 5)
    second_hop(blocks[6], 6)

    arrived(xb.at[0], o_sem)
    swap = rcopy(xb.at[0], xb.at[1], s_send, s_sem, sib)
    swap.start()
    deep_z(3)

    @pl.when(extra)
    def _():
        arrived(wb.at[0:54 * 16, 0:8 * HD], a_send)
        arrived(ob.at[:, 0:15 * ROWS, :], o_send)

    @pl.when(jnp.logical_not(extra))
    def _():
        arrived(wb.at[0:57 * 16, 0:8 * HD], a_send)
        arrived(ob.at[0, 0:15 * ROWS, :], o_send)

    own.wait()
    for slot in range(7):
        last_hop(blocks[slot], slot)
    arrived(deep(4, 0, RCH), zc_sem.at[3, 0])
    arrived(deep(4, RCH, RCH), zc_sem.at[3, 1])
    swap.wait()

    rows = xb[...].reshape(2 * ROWS, K)
    sends = []
    for step in range(DEPTH * NB // NC):
        cols = slice(step * NC, (step + 1) * NC)
        part = lax.dot_general(rows, wb[cols, :], (((1,), (1,)), ((), ())),
                               preferred_element_type=jnp.float32).astype(jnp.bfloat16)
        ys[:, cols] = part[ROWS:]
        send = rcopy(ys.at[:, cols], yb.at[c, :, cols], y_send.at[step], y_sem.at[step], sib)
        send.start()
        sends.append(send)
        yb[c, :, cols] = part[:ROWS]
    for send in sends:
        send.wait()
    for pair in range(DEPTH // 2):
        cols = slice(pair * 2 * NB, (pair + 1) * 2 * NB)
        a, b = yb[0, :, cols], yb[1, :, cols]
        out[:, pair * 4 * NB:(pair + 1) * 4 * NB] = jnp.concatenate(
            [a[:, :NB], b[:, :NB], a[:, NB:], b[:, NB:]], axis=1)
    arrived(wb.at[0:14 * RB + 7 * RC, :], w_send)


def per_device(queries, keys, values, block_masks, head_kind, out_weight):
    anywhere = pl.BlockSpec(memory_space=pl.ANY)
    vmem = pl.BlockSpec(memory_space=pltpu.VMEM)
    smem = pl.BlockSpec(memory_space=pltpu.SMEM)
    dma = pltpu.SemaphoreType.DMA
    bf16 = jnp.bfloat16
    attended = pl.pallas_call(
        kernel,
        out_shape=jax.ShapeDtypeStruct((ROWS, 2 * DEPTH * NB), bf16),
        in_specs=[anywhere, anywhere, anywhere, vmem, smem, anywhere],
        out_specs=vmem,
        scratch_shapes=[
            pltpu.VMEM((2, SEQ, HD), bf16),
            pltpu.VMEM((2, SEQ, HD), bf16),
            pltpu.VMEM((2, SEQ, 2 * HD), bf16),
            pltpu.VMEM((2, SEQ // HD, SEQ), jnp.float32),
            pltpu.VMEM((2, SEQ, HD), bf16),
            pltpu.VMEM((2, ROWS, K), bf16),
            pltpu.VMEM((DEPTH * NB, K), bf16),
            pltpu.VMEM((2, ROWS, DEPTH * NB), bf16),
            pltpu.VMEM((ROWS, DEPTH * NB), bf16),
            dma((4, 2, 2)), dma((4, 2)), dma((7, 2, 2)), dma((7, 2, 2)),
            dma((3, 2)), dma, dma, dma((DEPTH * NB // NC,)),
            dma, dma, dma, dma, dma((DEPTH * NB // NC,)), dma,
        ],
        compiler_params=pltpu.CompilerParams(
            collective_id=0, has_side_effects=True, vmem_limit_bytes=60 * 1024 * 1024),
    )(queries[0], keys[0], values[0], block_masks, head_kind, out_weight.T)
    return attended[None]


def solution(mesh):
    placed = (
        P("dp", "seq", None),
        P("dp", "seq", None),
        P("dp", "seq", None),
        P(),
        P(),
        P(None, "dp"),
    )
    return jax.shard_map(
        per_device, mesh=mesh, in_specs=placed, out_specs=P("dp", "seq", None), check_vma=False
    )
```

time: 176 us -> 105 us (0.60)
  Pallas kernels: 0 us -> 103 us
  waiting for transfers between devices: 42.9 us -> 0 us
  matrix products: 39.6 us -> 0 us
  local copies, waits for them, and re-layouts: 28.9 us -> 2.46 us
  blocking collectives: 19.2 us -> 0 us
  starting transfers between devices: 16.9 us -> 0 us
  between operations: 14.9 us -> 0.01 us
  other arithmetic: 6.61 us -> 0 us
  loops' own time: 5.96 us -> 0 us
    pallas_call x0 -> x1, Pallas kernels: none -> 103 us  [per_device(): pl.pallas_call(kernel, out_shape=jax.ShapeDtypeStruct((ROWS, 2 * DEPTH *...]
    dot_general x17 -> x0, matrix products: 39.6 us -> none  [the longest x8 17.3 us: one_block(): lax.dot_general(query_block, key_rows, (((1,), (1,)), ((), ())), preferre...]
    all_to_all x3 -> x0, waiting for transfers between devices: 37 us -> none  [the longest x1 14 us: per_device(): lax.all_to_all(arrange(key_heads), 'seq', split_axis=2, concat_axis=0, ti...]
    all_to_all x1 -> x0, blocking collectives: 19.2 us -> none  [per_device(): lax.all_to_all(stacked, 'seq', split_axis=0, concat_axis=2, tiled=True)]
    all_to_all x3 -> x0, starting transfers between devices: 16.9 us -> none  [the longest x1 7.72 us: per_device(): lax.all_to_all(arrange(key_heads), 'seq', split_axis=2, concat_axis=0, ti...]
    broadcast_in_dim x9 -> x0, local copies, waits for them, and re-layouts: 11.4 us -> none  [the longest x1 8.68 us: group_attention(): return jnp.stack(results, axis=1)[:, :, None, :]]
    reduce_sum x9 -> x0, other arithmetic: 6.4 us -> none  [the longest x8 5.69 us: one_block(): jnp.sum(powers, axis=1, keepdims=True)]
    another operation x2 -> x0, loops' own time: 5.96 us -> none  [attend(): outputs = lax.map(one_block, jnp.arange(count // step, dtype=jnp.int32))]
  transfers between devices with their start and end apart: 4 -> 0, of which waited for: 4 -> 0; matrix products, arithmetic and copies ran while one was open for 34% -> 0% of each run, Pallas kernels for 0% -> 0%
where the time goes in v1:
time: 105 us
  Pallas kernels  103 us (98%)
  local copies, waits for them, and re-layouts  2.46 us (2%)
    pallas_call x1, Pallas kernels, per_device(): pl.pallas_call(kernel, out_shape=jax.ShapeDtypeStruct((ROWS, 2 * DEPTH *...  103 us
    unnamed x1, local copies, waits for them, and re-layouts  2.46 us

profile of v1, /device:TPU:1, one launch (start us, length us, event | category | flops | bytes accessed | tf_op | source)
XLA Modules:
  0.0 105.2 jit_solution(15772493305575316594)
XLA Ops:
  0.0 102.8 %shard_map.64 = bf16[128,5120]{1,0:T(8,128)(2,1)} custom-call(bf16[128,2560]{1,0:T(8,128)(2,1)} %bitcast.7, bf16[128,2560]{1,0:T(8,128)(2,1)} %bitcast.8, bf16[128,2560]{1,0:T(8,128)(2,1)} %bitcast.9, s32[2,16,16]{2,1,0:T(8,128)} %masks.1, s32[20]{0:T(128)} %kinds.1, bf16[320,2560]{1,0:T(8,128)(2,1)} %bitcast.6), custom_call_target="tpu_custom_call" | custom-call | tf_op jit(solution)/shard_map/pallas_call | solution.py:285
  102.8 2.5 %copy.8 = bf16[1,128,5120]{2,1,0:T(8,128)(2,1)} copy(bf16[1,128,5120]{2,1,0:T(8,128)(2,1)} %bitcast.5) | data formatting | bytes 2621440

commit v2 on v1

--- a/solution.py
+++ b/solution.py
@@ -24,8 +24,12 @@
 RH = 64
 RCH = RC // 2
 QB = 256
+MB = SEQ // HD
+BIG = -1e30
 NC = 256
 MESH = pl.DeviceIdType.MESH
+ORDER = ((2, 2), (1, 0), (0, 1), (3, 0), (0, 3), (1, 2), (2, 1), (3, 2), (2, 3), (1, 1), (3, 3), (1, 3), (3, 1),
+         (2, 0), (0, 2))
 SCALE = math.log2(math.e) / math.sqrt(HD)
 
 
@@ -45,7 +49,7 @@
 
 
 def kernel(q_in, k_in, v_in, masks, kinds, w_in, out,
-           qb, kb, vb, bias, ob, xb, wb, yb, ys,
+           qb, kb, vb, sb, ob, xb, wb, yb, ys,
            zb_sem, zc_sem, x1_sem, x2_sem, a_sem, o_sem, s_sem, y_sem,
            w_send, a_send, o_send, s_send, y_send, l_sem):
     dp = lax.axis_index("dp")
@@ -60,8 +64,8 @@
         ((dp, xi * SIDE + (yi + 1) % SIDE), (dp, xi * SIDE + (yi + 3) % SIDE)),
     )
     coord = (xi, yi)
-    extra = me % 5 == 0
-    head1 = PLANE + me // 5
+    extra = yi == (xi + 2 * c) % SIDE
+    head1 = PLANE + xi
 
     barrier = pltpu.get_barrier_semaphore()
 
@@ -71,6 +75,22 @@
 
     for device in (up, down, sib):
         pl.semaphore_signal(barrier, inc=1, device_id=device, device_id_type=MESH)
+    own = pltpu.make_async_copy(w_in, wb.at[pl.ds(al(z * NB, 16), NB), :], l_sem)
+    own.start()
+
+    block = lax.broadcasted_iota(jnp.int32, (SEQ, HD), 0) // HD
+    lane = lax.broadcasted_iota(jnp.int32, (SEQ, HD), 1)
+    unit = jnp.where(block == lane, 1.0, 0.0).astype(jnp.bfloat16)
+    for slot in range(2):
+        kind = kinds[me if slot == 0 else jnp.where(extra, head1, me)]
+        allowed = jnp.where(kind == 0, masks[0], masks[1])
+        entries = jnp.where(allowed == 1, 0.0, BIG).astype(jnp.bfloat16)
+        kb[slot, :, HD:] = unit
+        vb[slot, :, HD:] = jnp.ones((SEQ, HD), jnp.bfloat16)
+        qb[slot, :, HD:] = jnp.zeros((SEQ, HD), jnp.bfloat16)
+        for row in range(MB):
+            qb[slot, row * HD:(row + 1) * HD, HD:HD + MB] = jnp.broadcast_to(entries[row:row + 1], (HD, MB))
+
     pl.semaphore_wait(barrier, PLANE + 2)
 
     def piece(block, kind, quarter, first=0, rows=RB):
@@ -80,9 +100,6 @@
     def deep(block, first, rows):
         start = al(((z + block) % DEPTH) * NB + 2 * RB + first, 16)
         return wb.at[pl.ds(start, rows), :]
-
-    own = pltpu.make_async_copy(w_in, wb.at[pl.ds(al(z * NB, 16), NB), :], l_sem)
-    own.start()
 
     for kind in range(2):
         src = w_in.at[kind * RB:(kind + 1) * RB, pl.ds(al(coord[kind] * KQ, HD), KQ)]
@@ -93,47 +110,34 @@
 
     def landing(which, slot, block):
         rows = pl.ds(al(block * ROWS, ROWS), ROWS)
-        if which == 2:
-            return vb.at[slot, rows, 0:HD]
-        return (kb, qb)[which].at[slot, rows, :]
+        return (kb, qb, vb)[which].at[slot, rows, 0:HD]
 
     def whole(which, slot):
-        if which == 2:
-            return vb.at[slot, :, 0:HD]
-        return (kb, qb)[which].at[slot]
+        return (kb, qb, vb)[which].at[slot, :, 0:HD]
 
     def columns(which, head):
         return sources[which].at[:, pl.ds(al(head * HD, HD), HD)]
 
-    @pl.loop(1, PLANE)
-    def _(d):
-        to = (me + d) % PLANE
+    for dx, dy in ORDER:
+        to = ((xi + dx) % SIDE) * SIDE + (yi + dy) % SIDE
         for which in range(3):
             rcopy(columns(which, to), landing(which, 0, me), a_send, a_sem.at[which, 0], (dp, to)).start()
 
     for which in range(3):
         pltpu.make_async_copy(columns(which, me), landing(which, 0, me), a_sem.at[which, 0]).start()
 
-    @pl.loop(0, EXTRA)
-    def _(j):
+    for j in range(EXTRA):
+        to = j * SIDE + (j + 2 * c) % SIDE
         for which in range(3):
-            @pl.when(me != 5 * j)
+            @pl.when(me != to)
             def _():
                 rcopy(columns(which, PLANE + j), landing(which, 1, me), a_send,
-                      a_sem.at[which, 1], (dp, 5 * j)).start()
-
-            @pl.when(me == 5 * j)
+                      a_sem.at[which, 1], (dp, to)).start()
+
+            @pl.when(me == to)
             def _():
                 pltpu.make_async_copy(columns(which, PLANE + j), landing(which, 1, me),
                                       a_sem.at[which, 1]).start()
-
-    for slot in range(2):
-        kind = kinds[me if slot == 0 else jnp.where(extra, head1, me)]
-        allowed = jnp.where(kind == 0, masks[0], masks[1])
-        for block in range(SEQ // HD):
-            column = jnp.where(allowed[:, block:block + 1] == 1, 0.0, -jnp.inf)
-            bias[slot, :, block * HD:(block + 1) * HD] = jnp.broadcast_to(column, (SEQ // HD, HD))
-        vb[slot, :, HD:] = jnp.ones((SEQ, HD), jnp.bfloat16)
 
     def first_hop(block, slot):
         for kind in range(2):
@@ -176,66 +180,90 @@
             part = deep(block, 0, RC) if step < 3 else deep(block, way * RCH, RCH)
             rcopy(part, part, w_send, zc_sem.at[step, way], (up, down)[way]).start()
 
+    def deep_first():
+        for way, device in enumerate((up, down)):
+            rcopy(w_in.at[2 * RB:NB, :], deep(DEPTH, 0, RC), w_send, zc_sem.at[0, way], device).start()
+
+    def along_z4():
+        for kind in range(2):
+            arrived(piece(4, kind, coord[kind]), zb_sem.at[3, kind, kind])
+        first_hop(4, 6)
+
+    steps = SEQ // QB
+
+    def rows_of(i):
+        turn = (i + me // 2) % steps
+        return turn, pl.ds(al(turn * QB, QB), QB)
+
+    def score(slot, i, place):
+        _, rows = rows_of(i)
+        sb[place] = lax.dot_general(qb[slot, rows, :], kb[slot], (((1,), (1,)), ((), ())),
+                                    preferred_element_type=jnp.float32)
+
+    def attend(slot, i, place):
+        head = jnp.where(slot == 0, me, head1)
+        turn, rows = rows_of(i)
+        scores = sb[place]
+        powers = jnp.exp2((scores - jnp.max(scores, axis=1, keepdims=True)) * SCALE).astype(jnp.bfloat16)
+        total = jnp.dot(powers, vb[slot], preferred_element_type=jnp.float32)
+        ob[slot, rows, :] = (total[:, :HD] / total[:, HD:]).astype(jnp.bfloat16)
+        for half in range(QB // ROWS):
+            to = turn * 2 + half
+            src = ob.at[slot, pl.ds(al(to * ROWS, ROWS), ROWS), :]
+            dst = xb.at[0, :, pl.ds(al(head * HD, HD), HD)]
+
+            @pl.when(to != me)
+            def _():
+                rcopy(src, dst, o_send, o_sem, (dp, to)).start()
+
+            @pl.when(to == me)
+            def _():
+                pltpu.make_async_copy(src, dst, o_sem).start()
+
     along_z(1)
     along_z(2)
     along_z(3)
-    for way, device in enumerate((up, down)):
-        rcopy(w_in.at[2 * RB:NB, :], deep(DEPTH, 0, RC), w_send, zc_sem.at[0, way], device).start()
-    for kind in range(2):
-        arrived(piece(4, kind, coord[kind]), zb_sem.at[3, kind, kind])
-    first_hop(4, 6)
-
-    def attention(slot, head, low, high):
-        @pl.loop(low, high)
-        def _(i):
-            turn = (i + me // 2) % (SEQ // QB)
-            rows = pl.ds(al(turn * QB, QB), QB)
-            scores = lax.dot_general(qb[slot, rows, :], kb[slot], (((1,), (1,)), ((), ())),
-                                     preferred_element_type=jnp.float32)
-            powers = []
-            for half in range(QB // ROWS):
-                part = scores[half * ROWS:(half + 1) * ROWS] + bias[slot, pl.ds(turn * 2 + half, 1), :]
-                largest = jnp.max(part, axis=1, keepdims=True)
-                powers.append(jnp.exp2((part - largest) * SCALE).astype(jnp.bfloat16))
-            total = jnp.dot(jnp.concatenate(powers, axis=0), vb[slot], preferred_element_type=jnp.float32)
-            ob[slot, rows, :] = (total[:, :HD] / total[:, HD:]).astype(jnp.bfloat16)
-            for half in range(QB // ROWS):
-                to = turn * 2 + half
-                src = ob.at[slot, pl.ds(al(to * ROWS, ROWS), ROWS), :]
-                dst = xb.at[0, :, pl.ds(al(head * HD, HD), HD)]
-
-                @pl.when(to != me)
-                def _():
-                    rcopy(src, dst, o_send, o_sem, (dp, to)).start()
-
-                @pl.when(to == me)
-                def _():
-                    pltpu.make_async_copy(src, dst, o_sem).start()
-
+    deep_first()
+    along_z4()
     for which in range(3):
         arrived(whole(which, 0), a_sem.at[which, 0])
-    attention(0, me, 0, 4)
+    score(0, 0, 0)
+
+    last = jnp.where(extra, steps, steps // 2) - 1
+
+    @pl.loop(0, last + 1)
+    def _(pair):
+        slot, i = pair // (steps // 2), 2 * (pair % (steps // 2))
+        score(slot, i + 1, 1)
+        attend(slot, i, 0)
+
+        @pl.when(jnp.logical_and(extra, pair == steps // 2 - 1))
+        def _():
+            for which in range(3):
+                arrived(whole(which, 1), a_sem.at[which, 1])
+
+        then = jnp.minimum(pair + 1, last)
+        score(then // (steps // 2), 2 * (then % (steps // 2)), 0)
+        attend(slot, i + 1, 1)
+
+        @pl.when(pair == 1)
+        def _():
+            deep_z(1)
+
+        @pl.when(pair == 3)
+        def _():
+            deep_z(2)
+
     second_hop(blocks[0], 0)
     second_hop(blocks[1], 1)
-    deep_z(1)
-    attention(0, me, 4, 8)
     second_hop(blocks[2], 2)
     second_hop(blocks[3], 3)
-
-    @pl.when(extra)
-    def _():
-        for which in range(3):
-            arrived(whole(which, 1), a_sem.at[which, 1])
-        attention(1, head1, 0, 8)
-
-    deep_z(2)
+    arrived(xb.at[0], o_sem)
+    swap = rcopy(xb.at[0], xb.at[1], s_send, s_sem, sib)
+    swap.start()
     second_hop(blocks[4], 4)
     second_hop(blocks[5], 5)
     second_hop(blocks[6], 6)
-
-    arrived(xb.at[0], o_sem)
-    swap = rcopy(xb.at[0], xb.at[1], s_send, s_sem, sib)
-    swap.start()
     deep_z(3)
 
     @pl.when(extra)
@@ -288,10 +316,10 @@
         in_specs=[anywhere, anywhere, anywhere, vmem, smem, anywhere],
         out_specs=vmem,
         scratch_shapes=[
-            pltpu.VMEM((2, SEQ, HD), bf16),
-            pltpu.VMEM((2, SEQ, HD), bf16),
             pltpu.VMEM((2, SEQ, 2 * HD), bf16),
-            pltpu.VMEM((2, SEQ // HD, SEQ), jnp.float32),
+            pltpu.VMEM((2, SEQ, 2 * HD), bf16),
+            pltpu.VMEM((2, SEQ, 2 * HD), bf16),
+            pltpu.VMEM((2, QB, SEQ), jnp.float32),
             pltpu.VMEM((2, SEQ, HD), bf16),
             pltpu.VMEM((2, ROWS, K), bf16),
             pltpu.VMEM((DEPTH * NB, K), bf16),

time: 105 us -> 92.6 us (0.88)
  Pallas kernels: 103 us -> 90 us
    pallas_call x1, Pallas kernels: 103 us -> 90 us  [per_device(): pl.pallas_call(kernel, out_shape=jax.ShapeDtypeStruct((ROWS, 2 * DEPTH *...]
where the time goes in v2:
time: 92.6 us; the launch traced here: 92.5 us
  Pallas kernels  90 us (97%)
  local copies, waits for them, and re-layouts  2.46 us (3%)
    pallas_call x1, Pallas kernels, per_device(): pl.pallas_call(kernel, out_shape=jax.ShapeDtypeStruct((ROWS, 2 * DEPTH *...  90 us
    unnamed x1, local copies, waits for them, and re-layouts  2.46 us

profile of v2, /device:TPU:1, one launch (start us, length us, event | category | flops | bytes accessed | tf_op | source)
XLA Modules:
  0.0 92.5 jit_solution(14197473171717369360)
XLA Ops:
  0.0 90.0 %shard_map.64 = bf16[128,5120]{1,0:T(8,128)(2,1)} custom-call(bf16[128,2560]{1,0:T(8,128)(2,1)} %bitcast.7, bf16[128,2560]{1,0:T(8,128)(2,1)} %bitcast.8, bf16[128,2560]{1,0:T(8,128)(2,1)} %bitcast.9, s32[2,16,16]{2,1,0:T(8,128)} %masks.1, s32[20]{0:T(128)} %kinds.1, bf16[320,2560]{1,0:T(8,128)(2,1)} %bitcast.6), custom_call_target="tpu_custom_call" | custom-call | tf_op jit(solution)/shard_map/pallas_call | solution.py:313
  90.0 2.5 %copy.8 = bf16[1,128,5120]{2,1,0:T(8,128)(2,1)} copy(bf16[1,128,5120]{2,1,0:T(8,128)(2,1)} %bitcast.5) | data formatting | bytes 2621440

commit v3 on v2

--- a/solution.py
+++ b/solution.py
@@ -26,7 +26,6 @@
 QB = 256
 MB = SEQ // HD
 BIG = -1e30
-NC = 256
 MESH = pl.DeviceIdType.MESH
 ORDER = ((2, 2), (1, 0), (0, 1), (3, 0), (0, 3), (1, 2), (2, 1), (3, 2), (2, 3), (1, 1), (3, 3), (1, 3), (3, 1),
          (2, 0), (0, 2))
@@ -171,23 +170,23 @@
                 if step < 3 or kind == way:
                     part = piece(block, kind, coord[kind])
                     rcopy(part, part, w_send, zb_sem.at[step, way, kind], (up, down)[way]).start()
-            first_hop(block, 2 * (step - 1) + way)
-
-    def deep_z(step):
+
+    def deep_z(step, half):
         for way in range(2):
-            block = (DEPTH - step, step)[way]
-            arrived(deep(block, 0, RC), zc_sem.at[step - 1, way])
-            part = deep(block, 0, RC) if step < 3 else deep(block, way * RCH, RCH)
-            rcopy(part, part, w_send, zc_sem.at[step, way], (up, down)[way]).start()
+            part = deep((DEPTH - step, step)[way], half * RCH, RCH)
+            arrived(part, zc_sem.at[step - 1, way, half])
+            if step < 3 or half == way:
+                rcopy(part, part, w_send, zc_sem.at[step, way, half], (up, down)[way]).start()
 
     def deep_first():
-        for way, device in enumerate((up, down)):
-            rcopy(w_in.at[2 * RB:NB, :], deep(DEPTH, 0, RC), w_send, zc_sem.at[0, way], device).start()
+        for half in range(2):
+            for way, device in enumerate((up, down)):
+                src = w_in.at[2 * RB + half * RCH:2 * RB + (half + 1) * RCH, :]
+                rcopy(src, deep(DEPTH, half * RCH, RCH), w_send, zc_sem.at[0, way, half], device).start()
 
     def along_z4():
         for kind in range(2):
             arrived(piece(4, kind, coord[kind]), zb_sem.at[3, kind, kind])
-        first_hop(4, 6)
 
     steps = SEQ // QB
 
@@ -221,10 +220,17 @@
                 pltpu.make_async_copy(src, dst, o_sem).start()
 
     along_z(1)
+    first_hop(blocks[0], 0)
+    first_hop(blocks[1], 1)
     along_z(2)
+    first_hop(blocks[2], 2)
+    first_hop(blocks[3], 3)
     along_z(3)
+    first_hop(blocks[4], 4)
+    first_hop(blocks[5], 5)
     deep_first()
     along_z4()
+    first_hop(blocks[6], 6)
     for which in range(3):
         arrived(whole(which, 0), a_sem.at[which, 0])
     score(0, 0, 0)
@@ -248,12 +254,17 @@
 
         @pl.when(pair == 1)
         def _():
-            deep_z(1)
+            deep_z(1, 0)
+
+        @pl.when(pair == 2)
+        def _():
+            deep_z(1, 1)
 
         @pl.when(pair == 3)
         def _():
-            deep_z(2)
-
+            deep_z(2, 0)
+
+    deep_z(2, 1)
     second_hop(blocks[0], 0)
     second_hop(blocks[1], 1)
     second_hop(blocks[2], 2)
@@ -261,10 +272,53 @@
     arrived(xb.at[0], o_sem)
     swap = rcopy(xb.at[0], xb.at[1], s_send, s_sem, sib)
     swap.start()
+    deep_z(3, 0)
     second_hop(blocks[4], 4)
     second_hop(blocks[5], 5)
+    own.wait()
+    swap.wait()
+
+    rows = xb[...].reshape(2 * ROWS, K)
+
+    def project(slot, block):
+        where = (z + block) % DEPTH
+        part = lax.dot_general(rows, wb[pl.ds(al(where * NB, 64), NB), :], (((1,), (1,)), ((), ())),
+                               preferred_element_type=jnp.float32).astype(jnp.bfloat16)
+        ys[slot] = part[ROWS:]
+        rcopy(ys.at[slot], yb.at[c, slot], y_send.at[slot], y_sem.at[slot], sib).start()
+        yb[c, slot] = part[:ROWS]
+
+    def assemble(slot, block):
+        where = (z + block) % DEPTH
+        arrived(yb.at[1 - c, slot], y_sem.at[slot])
+        out[:, pl.ds(al(where * 2 * NB, HD), 2 * NB)] = jnp.concatenate([yb[0, slot], yb[1, slot]], axis=1)
+
+    project(7, 0)
+    last_hop(blocks[0], 0)
+    project(0, blocks[0])
+    assemble(7, 0)
+    deep_z(3, 1)
     second_hop(blocks[6], 6)
-    deep_z(3)
+    last_hop(blocks[1], 1)
+    project(1, blocks[1])
+    assemble(0, blocks[0])
+    last_hop(blocks[2], 2)
+    project(2, blocks[2])
+    assemble(1, blocks[1])
+    last_hop(blocks[3], 3)
+    project(3, blocks[3])
+    assemble(2, blocks[2])
+    last_hop(blocks[4], 4)
+    project(4, blocks[4])
+    assemble(3, blocks[3])
+    last_hop(blocks[5], 5)
+    project(5, blocks[5])
+    assemble(4, blocks[4])
+    last_hop(blocks[6], 6)
+    arrived(deep(4, 0, RCH), zc_sem.at[3, 0, 0])
+    arrived(deep(4, RCH, RCH), zc_sem.at[3, 1, 1])
+    project(6, blocks[6])
+    assemble(5, blocks[5])
 
     @pl.when(extra)
     def _():
@@ -275,33 +329,10 @@
     def _():
         arrived(wb.at[0:57 * 16, 0:8 * HD], a_send)
         arrived(ob.at[0, 0:15 * ROWS, :], o_send)
-
-    own.wait()
-    for slot in range(7):
-        last_hop(blocks[slot], slot)
-    arrived(deep(4, 0, RCH), zc_sem.at[3, 0])
-    arrived(deep(4, RCH, RCH), zc_sem.at[3, 1])
-    swap.wait()
-
-    rows = xb[...].reshape(2 * ROWS, K)
-    sends = []
-    for step in range(DEPTH * NB // NC):
-        cols = slice(step * NC, (step + 1) * NC)
-        part = lax.dot_general(rows, wb[cols, :], (((1,), (1,)), ((), ())),
-                               preferred_element_type=jnp.float32).astype(jnp.bfloat16)
-        ys[:, cols] = part[ROWS:]
-        send = rcopy(ys.at[:, cols], yb.at[c, :, cols], y_send.at[step], y_sem.at[step], sib)
-        send.start()
-        sends.append(send)
-        yb[c, :, cols] = part[:ROWS]
-    for send in sends:
-        send.wait()
-    for pair in range(DEPTH // 2):
-        cols = slice(pair * 2 * NB, (pair + 1) * 2 * NB)
-        a, b = yb[0, :, cols], yb[1, :, cols]
-        out[:, pair * 4 * NB:(pair + 1) * 4 * NB] = jnp.concatenate(
-            [a[:, :NB], b[:, :NB], a[:, NB:], b[:, NB:]], axis=1)
     arrived(wb.at[0:14 * RB + 7 * RC, :], w_send)
+    assemble(6, blocks[6])
+    for slot in range(DEPTH):
+        arrived(ys.at[slot], y_send.at[slot])
 
 
 def per_device(queries, keys, values, block_masks, head_kind, out_weight):
@@ -323,11 +354,11 @@
             pltpu.VMEM((2, SEQ, HD), bf16),
             pltpu.VMEM((2, ROWS, K), bf16),
             pltpu.VMEM((DEPTH * NB, K), bf16),
-            pltpu.VMEM((2, ROWS, DEPTH * NB), bf16),
-            pltpu.VMEM((ROWS, DEPTH * NB), bf16),
-            dma((4, 2, 2)), dma((4, 2)), dma((7, 2, 2)), dma((7, 2, 2)),
-            dma((3, 2)), dma, dma, dma((DEPTH * NB // NC,)),
-            dma, dma, dma, dma, dma((DEPTH * NB // NC,)), dma,
+            pltpu.VMEM((2, DEPTH, ROWS, NB), bf16),
+            pltpu.VMEM((DEPTH, ROWS, NB), bf16),
+            dma((4, 2, 2)), dma((4, 2, 2)), dma((7, 2, 2)), dma((7, 2, 2)),
+            dma((3, 2)), dma, dma, dma((DEPTH,)),
+            dma, dma, dma, dma, dma((DEPTH,)), dma,
         ],
         compiler_params=pltpu.CompilerParams(
             collective_id=0, has_side_effects=True, vmem_limit_bytes=60 * 1024 * 1024),

time: 92.6 us -> 84.9 us (0.917)
  Pallas kernels: 90 us -> 82.2 us
    pallas_call x1, Pallas kernels: 90 us -> 82.2 us  [per_device(): pl.pallas_call(kernel, out_shape=jax.ShapeDtypeStruct((ROWS, 2 * DEPTH *...]
where the time goes in v3:
time: 84.9 us; the launch traced here: 84.7 us
  Pallas kernels  82.2 us (97%)
  local copies, waits for them, and re-layouts  2.46 us (3%)
    pallas_call x1, Pallas kernels, per_device(): pl.pallas_call(kernel, out_shape=jax.ShapeDtypeStruct((ROWS, 2 * DEPTH *...  82.2 us
    unnamed x1, local copies, waits for them, and re-layouts  2.46 us

profile of v3, /device:TPU:1, one launch (start us, length us, event | category | flops | bytes accessed | tf_op | source)
XLA Modules:
  0.0 84.7 jit_solution(74838853180394655)
XLA Ops:
  0.0 82.2 %shard_map.64 = bf16[128,5120]{1,0:T(8,128)(2,1)} custom-call(bf16[128,2560]{1,0:T(8,128)(2,1)} %bitcast.7, bf16[128,2560]{1,0:T(8,128)(2,1)} %bitcast.8, bf16[128,2560]{1,0:T(8,128)(2,1)} %bitcast.9, s32[2,16,16]{2,1,0:T(8,128)} %masks.1, s32[20]{0:T(128)} %kinds.1, bf16[320,2560]{1,0:T(8,128)(2,1)} %bitcast.6), custom_call_target="tpu_custom_call" | custom-call | tf_op jit(solution)/shard_map/pallas_call | solution.py:344
  82.2 2.5 %copy.8 = bf16[1,128,5120]{2,1,0:T(8,128)(2,1)} copy(bf16[1,128,5120]{2,1,0:T(8,128)(2,1)} %bitcast.5) | data formatting | bytes 2621440

commit v4 on v3

--- a/solution.py
+++ b/solution.py
@@ -47,8 +47,8 @@
     return pl.multiple_of(value, unit)
 
 
-def kernel(q_in, k_in, v_in, masks, kinds, w_in, out,
-           qb, kb, vb, sb, ob, xb, wb, yb, ys,
+def kernel(q_in, k_in, v_in, masks, kinds, w_in, result,
+           out, r_sem, qb, kb, vb, sb, ob, xb, wb, yb, ys,
            zb_sem, zc_sem, x1_sem, x2_sem, a_sem, o_sem, s_sem, y_sem,
            w_send, a_send, o_send, s_send, y_send, l_sem):
     dp = lax.axis_index("dp")
@@ -213,11 +213,11 @@
 
             @pl.when(to != me)
             def _():
-                rcopy(src, dst, o_send, o_sem, (dp, to)).start()
+                rcopy(src, dst, o_send, o_sem.at[slot], (dp, to)).start()
 
             @pl.when(to == me)
             def _():
-                pltpu.make_async_copy(src, dst, o_sem).start()
+                pltpu.make_async_copy(src, dst, o_sem.at[slot]).start()
 
     along_z(1)
     first_hop(blocks[0], 0)
@@ -269,14 +269,18 @@
     second_hop(blocks[1], 1)
     second_hop(blocks[2], 2)
     second_hop(blocks[3], 3)
-    arrived(xb.at[0], o_sem)
-    swap = rcopy(xb.at[0], xb.at[1], s_send, s_sem, sib)
-    swap.start()
+    swaps = []
+    for slot, cols in enumerate((slice(0, PLANE * HD), slice(PLANE * HD, K))):
+        arrived(xb.at[0, :, cols], o_sem.at[slot])
+        swap = rcopy(xb.at[0, :, cols], xb.at[1, :, cols], s_send.at[slot], s_sem.at[slot], sib)
+        swap.start()
+        swaps.append(swap)
     deep_z(3, 0)
     second_hop(blocks[4], 4)
     second_hop(blocks[5], 5)
     own.wait()
-    swap.wait()
+    for swap in swaps:
+        swap.wait()
 
     rows = xb[...].reshape(2 * ROWS, K)
 
@@ -291,7 +295,8 @@
     def assemble(slot, block):
         where = (z + block) % DEPTH
         arrived(yb.at[1 - c, slot], y_sem.at[slot])
-        out[:, pl.ds(al(where * 2 * NB, HD), 2 * NB)] = jnp.concatenate([yb[0, slot], yb[1, slot]], axis=1)
+        out[slot] = jnp.concatenate([yb[0, slot], yb[1, slot]], axis=1)
+        pltpu.make_async_copy(out.at[slot], result.at[:, pl.ds(al(where * 2 * NB, HD), 2 * NB)], r_sem.at[slot]).start()
 
     project(7, 0)
     last_hop(blocks[0], 0)
@@ -333,6 +338,7 @@
     assemble(6, blocks[6])
     for slot in range(DEPTH):
         arrived(ys.at[slot], y_send.at[slot])
+        arrived(out.at[slot], r_sem.at[slot])
 
 
 def per_device(queries, keys, values, block_masks, head_kind, out_weight):
@@ -345,8 +351,9 @@
         kernel,
         out_shape=jax.ShapeDtypeStruct((ROWS, 2 * DEPTH * NB), bf16),
         in_specs=[anywhere, anywhere, anywhere, vmem, smem, anywhere],
-        out_specs=vmem,
+        out_specs=anywhere,
         scratch_shapes=[
+            pltpu.VMEM((DEPTH, ROWS, 2 * NB), bf16), dma((DEPTH,)),
             pltpu.VMEM((2, SEQ, 2 * HD), bf16),
             pltpu.VMEM((2, SEQ, 2 * HD), bf16),
             pltpu.VMEM((2, SEQ, 2 * HD), bf16),
@@ -357,8 +364,8 @@
             pltpu.VMEM((2, DEPTH, ROWS, NB), bf16),
             pltpu.VMEM((DEPTH, ROWS, NB), bf16),
             dma((4, 2, 2)), dma((4, 2, 2)), dma((7, 2, 2)), dma((7, 2, 2)),
-            dma((3, 2)), dma, dma, dma((DEPTH,)),
-            dma, dma, dma, dma, dma((DEPTH,)), dma,
+            dma((3, 2)), dma((2,)), dma((2,)), dma((DEPTH,)),
+            dma, dma, dma, dma((2,)), dma((DEPTH,)), dma,
         ],
         compiler_params=pltpu.CompilerParams(
             collective_id=0, has_side_effects=True, vmem_limit_bytes=60 * 1024 * 1024),

time: 84.9 us -> 84.5 us (level)
  no operation moved by 1% of the time
where the time goes in v4:
time: 84.5 us; the launch traced here: 84.4 us
  Pallas kernels  81.9 us (97%)
  local copies, waits for them, and re-layouts  2.46 us (3%)
    pallas_call x1, Pallas kernels, per_device(): pl.pallas_call(kernel, out_shape=jax.ShapeDtypeStruct((ROWS, 2 * DEPTH *...  81.9 us
    unnamed x1, local copies, waits for them, and re-layouts  2.46 us

profile of v4, /device:TPU:1, one launch (start us, length us, event | category | flops | bytes accessed | tf_op | source)
XLA Modules:
  0.0 84.4 jit_solution(15122245334739747037)
XLA Ops:
  0.0 81.9 %shard_map.64 = bf16[128,5120]{1,0:T(8,128)(2,1)} custom-call(bf16[128,2560]{1,0:T(8,128)(2,1)} %bitcast.7, bf16[128,2560]{1,0:T(8,128)(2,1)} %bitcast.8, bf16[128,2560]{1,0:T(8,128)(2,1)} %bitcast.9, s32[2,16,16]{2,1,0:T(8,128)} %masks.1, s32[20]{0:T(128)} %kinds.1, bf16[320,2560]{1,0:T(8,128)(2,1)} %bitcast.6), custom_call_target="tpu_custom_call" | custom-call | tf_op jit(solution)/shard_map/pallas_call | solution.py:350
  81.9 2.5 %copy.8 = bf16[1,128,5120]{2,1,0:T(8,128)(2,1)} copy(bf16[1,128,5120]{2,1,0:T(8,128)(2,1)} %bitcast.5) | data formatting | bytes 2621440

commit v5 on v4

--- a/solution.py
+++ b/solution.py
@@ -276,6 +276,7 @@
         swap.start()
         swaps.append(swap)
     deep_z(3, 0)
+    deep_z(3, 1)
     second_hop(blocks[4], 4)
     second_hop(blocks[5], 5)
     own.wait()
@@ -302,7 +303,6 @@
     last_hop(blocks[0], 0)
     project(0, blocks[0])
     assemble(7, 0)
-    deep_z(3, 1)
     second_hop(blocks[6], 6)
     last_hop(blocks[1], 1)
     project(1, blocks[1])

time: 84.5 us -> 84.5 us (level)
  no operation moved by 1% of the time
where the time goes in v5:
time: 84.5 us; the launch traced here: 84.4 us
  Pallas kernels  81.9 us (97%)
  local copies, waits for them, and re-layouts  2.46 us (3%)
    pallas_call x1, Pallas kernels, per_device(): pl.pallas_call(kernel, out_shape=jax.ShapeDtypeStruct((ROWS, 2 * DEPTH *...  81.9 us
    unnamed x1, local copies, waits for them, and re-layouts  2.46 us

profile of v5, /device:TPU:1, one launch (start us, length us, event | category | flops | bytes accessed | tf_op | source)
XLA Modules:
  0.0 84.4 jit_solution(1104095880339215473)
XLA Ops:
  0.0 81.9 %shard_map.64 = bf16[128,5120]{1,0:T(8,128)(2,1)} custom-call(bf16[128,2560]{1,0:T(8,128)(2,1)} %bitcast.7, bf16[128,2560]{1,0:T(8,128)(2,1)} %bitcast.8, bf16[128,2560]{1,0:T(8,128)(2,1)} %bitcast.9, s32[2,16,16]{2,1,0:T(8,128)} %masks.1, s32[20]{0:T(128)} %kinds.1, bf16[320,2560]{1,0:T(8,128)(2,1)} %bitcast.6), custom_call_target="tpu_custom_call" | custom-call | tf_op jit(solution)/shard_map/pallas_call | solution.py:350
  81.9 2.5 %copy.8 = bf16[1,128,5120]{2,1,0:T(8,128)(2,1)} copy(bf16[1,128,5120]{2,1,0:T(8,128)(2,1)} %bitcast.5) | data formatting | bytes 2621440

commit v6 on v5

--- a/solution.py
+++ b/solution.py
@@ -299,11 +299,11 @@
         out[slot] = jnp.concatenate([yb[0, slot], yb[1, slot]], axis=1)
         pltpu.make_async_copy(out.at[slot], result.at[:, pl.ds(al(where * 2 * NB, HD), 2 * NB)], r_sem.at[slot]).start()
 
+    second_hop(blocks[6], 6)
     project(7, 0)
     last_hop(blocks[0], 0)
     project(0, blocks[0])
     assemble(7, 0)
-    second_hop(blocks[6], 6)
     last_hop(blocks[1], 1)
     project(1, blocks[1])
     assemble(0, blocks[0])

time: 84.5 us -> 84.5 us (level)
  no operation moved by 1% of the time
where the time goes in v6:
time: 84.5 us; the launch traced here: 84.4 us
  Pallas kernels  81.9 us (97%)
  local copies, waits for them, and re-layouts  2.46 us (3%)
    pallas_call x1, Pallas kernels, per_device(): pl.pallas_call(kernel, out_shape=jax.ShapeDtypeStruct((ROWS, 2 * DEPTH *...  81.9 us
    unnamed x1, local copies, waits for them, and re-layouts  2.46 us

profile of v6, /device:TPU:1, one launch (start us, length us, event | category | flops | bytes accessed | tf_op | source)
XLA Modules:
  0.0 84.4 jit_solution(15302062500290857385)
XLA Ops:
  0.0 81.9 %shard_map.64 = bf16[128,5120]{1,0:T(8,128)(2,1)} custom-call(bf16[128,2560]{1,0:T(8,128)(2,1)} %bitcast.7, bf16[128,2560]{1,0:T(8,128)(2,1)} %bitcast.8, bf16[128,2560]{1,0:T(8,128)(2,1)} %bitcast.9, s32[2,16,16]{2,1,0:T(8,128)} %masks.1, s32[20]{0:T(128)} %kinds.1, bf16[320,2560]{1,0:T(8,128)(2,1)} %bitcast.6), custom_call_target="tpu_custom_call" | custom-call | tf_op jit(solution)/shard_map/pallas_call | solution.py:350
  81.9 2.5 %copy.8 = bf16[1,128,5120]{2,1,0:T(8,128)(2,1)} copy(bf16[1,128,5120]{2,1,0:T(8,128)(2,1)} %bitcast.5) | data formatting | bytes 2621440
